TPU v7x, 128 devices: a whole 4x4x4 slice. The times are simulated.
128 devices in a mesh: pb: 8 (over z_hi, x), ta: 16 (over z_lo, y, core).
Axes of the slice: x: 4, y: 4, z: 4 (z_hi: 2, z_lo: 2; z = z_hi * 2 + z_lo), core: 2. Of those that a mesh axis runs over, the one named last changes fastest.
Arguments:
- green: bfloat16 [8, 128, 256, 256], P(None, 'ta'), may hold values from -0.00059890747 to 0.00059890747
- colloc: bfloat16 [8, 384, 256], replicated, may hold values from -0.375 to 0.375
- kplus: int32 [8, 8], replicated, may hold values from 0 to 7, as said below
- to_freq: bfloat16 [128, 128], replicated, may hold values from -0.5 to 0.5
- to_time: bfloat16 [128, 128], replicated, may hold values from -0.5 to 0.5
- coulomb: bfloat16 [384, 384], replicated, may hold values from -438272 to 438272
Outputs:
- sigma: float32 [8, 128, 256, 256], P('pb', 'ta')
Inputs may be any that keep to these rules, and one draw needn't show every extreme that they name: kplus is the addition table of a periodic mesh of 8 points numbered in some order: every row and every column is a permutation, and kplus[q, kplus[r, k]] = kplus[kplus[q, r], k]; row q is the transfer numbered q.
All inputs are finite; a program needn't handle non-finite values.
Results may differ from a plain program's by a relative error of at most 0.023.
Values may be sent and summed in bfloat16 or wider, within the bound.
A program may use at most 256 MiB of HBM per device.

v0:
```python
import jax
import jax.numpy as jnp
from jax import lax
from jax.sharding import PartitionSpec as P


def swap_pairs(values):
    shape = values.shape
    paired = values.reshape(shape[0], shape[1] // 2, 2, shape[2], shape[3])
    return paired[:, :, ::-1].reshape(shape)


def local(green, colloc, kplus, to_freq, to_time, coulomb):
    npoints = green.shape[0]
    scale = -1.0 / npoints
    half_proj = jnp.einsum(
        "ktij,kqj->ktiq", green, colloc, preferred_element_type=jnp.float32
    ).astype(jnp.bfloat16)
    aux_green = jnp.einsum(
        "kpi,ktiq->ktpq", colloc, half_proj, preferred_element_type=jnp.float32
    ).astype(jnp.bfloat16)
    mirror = swap_pairs(aux_green)
    own_group = lax.axis_index("pb")
    plus_row = lax.dynamic_slice_in_dim(kplus, own_group, 1, 0)[0]
    shifted = jnp.take(aux_green, plus_row, axis=0)
    polar = (
        scale * jnp.einsum("ktpq,ktqp->tpq", shifted, mirror, preferred_element_type=jnp.float32)
    ).astype(jnp.bfloat16)
    freq_block = jnp.einsum(
        "wt,tpq->wpq",
        to_freq,
        lax.all_to_all(polar, "ta", split_axis=1, concat_axis=0, tiled=True),
        preferred_element_type=jnp.float32,
    ).astype(jnp.bfloat16)
    freq_polar = lax.all_to_all(freq_block, "ta", split_axis=0, concat_axis=1, tiled=True)
    first = jnp.einsum(
        "wpr,rq->wpq", freq_polar, coulomb, preferred_element_type=jnp.float32
    ).astype(jnp.bfloat16)
    series = (
        freq_polar.astype(jnp.float32)
        + jnp.einsum("wpr,wrq->wpq", first, freq_polar, preferred_element_type=jnp.float32)
    ).astype(jnp.bfloat16)
    left_prod = jnp.einsum(
        "pr,wrq->wpq", coulomb, series, preferred_element_type=jnp.float32
    ).astype(jnp.bfloat16)
    screen_freq = jnp.einsum(
        "wpr,rq->wpq", left_prod, coulomb, preferred_element_type=jnp.float32
    ).astype(jnp.bfloat16)
    time_block = jnp.einsum(
        "tw,wpq->tpq",
        to_time,
        lax.all_to_all(screen_freq, "ta", split_axis=1, concat_axis=0, tiled=True),
        preferred_element_type=jnp.float32,
    ).astype(jnp.bfloat16)
    screen_time = lax.all_to_all(time_block, "ta", split_axis=0, concat_axis=1, tiled=True)
    point_ids = jnp.arange(npoints, dtype=jnp.int32)
    sources = jnp.sum(
        jnp.where(plus_row[None, :] == point_ids[:, None], point_ids[None, :], 0), axis=1
    )
    chosen = jnp.take(aux_green, sources, axis=0)
    hadamard = (chosen.astype(jnp.float32) * screen_time[None].astype(jnp.float32)).astype(
        jnp.bfloat16
    )
    right_prod = jnp.einsum("ktpq,kqj->ktpj", hadamard, colloc, preferred_element_type=jnp.float32)
    return lax.psum_scatter(
        (
            scale
            * jnp.einsum(
                "kpi,ktpj->ktij",
                colloc.astype(jnp.float32),
                right_prod,
                precision=lax.Precision.HIGHEST,
            )
        ).astype(jnp.bfloat16),
        "pb",
        scatter_dimension=0,
        tiled=True,
    ).astype(jnp.float32)


def solution(mesh):
    in_specs = (P(None, "ta", None, None), P(), P(), P(), P(), P())
    out_specs = P("pb", "ta", None, None)
    return jax.shard_map(local, mesh=mesh, in_specs=in_specs, out_specs=out_specs, check_vma=False)
```

profile of v0, /device:TPU:1, one launch (start us, length us, event | category | flops | bytes accessed | tf_op | source)
XLA Modules:
  0.0 500.3 jit_solution(13744721614656089873)
XLA Ops:
  6.5 0.0 copy-start
  6.5 1.4 copy-done
  7.9 15.7 %fusion.9 = bf16[8,8,384,384]{3,2,1,0:T(8,128)(2,1)} fusion(bf16[8,8,256,256]{3,2,1,0:T(8,128)(2,1)} %param.8, bf16[8,384,256]{2,1,0:T(8,128)(2,1)S(1)} %copy-done), kind=kOutput, calls=%fused_computation.18 | convolution fusion | flops 8068792320 | bytes 28835840 | tf_op jit(solution)/shard_map/kpi,ktiq->ktpq/dot_general | solution.py:19
  23.6 6.1 %mini-gather-slice.9 = bf16[8,8,128,384]{2,3,1,0:T(8,128)(2,1)} slice(bf16[8,8,384,384]{2,3,1,0:T(8,128)(2,1)} %bitcast.69), slice={[0:8], [0:8], [256:384], [0:384]} | slice | bytes 12582912 | tf_op jit(solution)/shard_map/jit(_take)/gather | solution.py:60
  29.7 10.6 %mini-gather-slice.8 = bf16[8,8,256,384]{2,3,1,0:T(8,128)(2,1)} slice(bf16[8,8,384,384]{2,3,1,0:T(8,128)(2,1)} %bitcast.70), slice={[0:8], [0:8], [0:256], [0:384]} | slice | bytes 25165824 | tf_op jit(solution)/shard_map/jit(_take)/gather | solution.py:60
  40.3 0.7 compare_and_fusion
  41.1 6.7 %gather_fusion.3 = bf16[8,8,128,384]{2,3,1,0:T(8,128)(2,1)} fusion(bf16[8,8,128,384]{2,3,1,0:T(8,128)(2,1)} %mini-gather-slice.9, s32[1024]{0:T(1024)S(1)} %pad_clamp_fusion), kind=kCustom, calls=%fused_computation.3.clone | custom fusion | bytes 12582944 | tf_op jit(solution)/shard_map/jit(_take)/gather | solution.py:25
  47.8 10.9 %gather_fusion.2 = bf16[8,8,256,384]{2,3,1,0:T(8,128)(2,1)} fusion(bf16[8,8,256,384]{2,3,1,0:T(8,128)(2,1)} %mini-gather-slice.8, s32[1024]{0:T(1024)S(1)} %pad_clamp_fusion), kind=kCustom, calls=%fused_computation.2.clone | custom fusion | bytes 25165856 | tf_op jit(solution)/shard_map/jit(_take)/gather | solution.py:25
  58.7 20.4 %fusion.4 = f32[8,384,384,8]{1,2,0,3:T(8,128)} fusion(bf16[8,8,128,384]{2,3,1,0:T(8,128)(2,1)} %gather_fusion.3, bf16[8,8,256,384]{2,3,1,0:T(8,128)(2,1)} %gather_fusion.2, pred[8]{0:T(512)(128)(4,1)S(1)} %get-tuple-element.6), kind=kLoop, calls=%fused_computation.12 | loop fusion | flops 56623104 | bytes 56623112
  79.1 36.7 %copy.79 = f32[8,384,384,8]{2,1,0,3:T(8,128)} copy(f32[8,384,384,8]{1,2,0,3:T(8,128)} %fusion.4) | data formatting | bytes 75497472
  115.8 18.8 %rev.3 = bf16[8,4,2,384,384]{3,4,2,1,0:T(8,128)(2,1)} reverse(bf16[8,4,2,384,384]{3,4,2,1,0:T(8,128)(2,1)} %bitcast.71), dimensions={2} | reverse | bytes 37748736 | tf_op jit(solution)/shard_map/rev | solution.py:10
  134.7 18.6 %multiply_reduce_fusion = f32[8,384,384]{2,1,0:T(8,128)S(1)} fusion(f32[8,384,384,8]{2,1,0,3:T(8,128)} %copy.79, bf16[8,384,384,8]{2,1,0,3:T(8,128)(2,1)} %bitcast.72), kind=kLoop, calls=%fused_computation.4 | loop fusion | flops 27131904 | bytes 61341696
  153.2 2.7 fusion.16
  155.9 0.0 copy-start.3
  155.9 36.8 %all_to_all.63 = bf16[8,384,384]{2,0,1:T(8,128)(2,1)S(1)} all-to-all(bf16[8,384,384]{2,0,1:T(8,128)(2,1)S(1)} %fusion.16), channel_id=1, replica_groups=mesh['pb'=8,'ta'=16] {'ta'}, dimensions={1} | all-to-all | bytes 4718592 | tf_op jit(solution)/shard_map/all_to_all | solution.py:32
  192.7 0.4 copy.56
  193.2 0.0 copy-done.3
  193.2 2.2 convert_bitcast_fusion.2
  195.4 4.6 copy.58
  200.0 34.0 %all_to_all.64 = bf16[128,24,384]{2,1,0:T(8,128)(2,1)S(1)} all-to-all(bf16[128,24,384]{2,1,0:T(8,128)(2,1)} %copy.58), channel_id=1, replica_groups=mesh['pb'=8,'ta'=16] {'ta'}, dimensions={0} | all-to-all | bytes 4718592 | tf_op jit(solution)/shard_map/all_to_all | solution.py:35
  234.0 0.3 copy.59
  234.3 0.0 copy-start.1
  234.3 1.4 copy-done.1
  235.7 0.0 copy-done.2
  235.7 3.0 fusion.44
  238.8 7.6 %fusion.17 = bf16[8,384,384]{2,1,0:T(8,128)(2,1)} fusion(bf16[8,384,384]{2,1,0:T(8,128)(2,1)} %bitcast.75, bf16[8,384,384]{2,1,0:T(8,128)(2,1)} %fusion.44, bf16[384,384]{1,0:T(8,128)(2,1)S(1)} %copy-done.2), kind=kOutput, calls=%fused_computation.26 | convolution fusion | flops 1815478272 | bytes 7372800 | tf_op jit(solution)/shard_map/pr,wrq->wpq/dot_general | solution.py:43
  246.3 3.3 fusion.35
  249.6 0.0 copy-start.4
  249.6 1.4 copy.62
  251.0 33.0 %all_to_all.65 = bf16[8,384,384]{2,0,1:T(8,128)(2,1)S(1)} all-to-all(bf16[8,384,384]{2,0,1:T(8,128)(2,1)S(1)} %copy.62), channel_id=1, replica_groups=mesh['pb'=8,'ta'=16] {'ta'}, dimensions={1} | all-to-all | bytes 4718592 | tf_op jit(solution)/shard_map/all_to_all | solution.py:52
  284.0 0.4 copy.64
  284.5 0.0 copy-done.4
  284.5 2.2 convert_bitcast_fusion.1
  286.7 4.5 copy.66
  291.2 5.0 all-to-all-start.3
  296.2 0.3 reduce-scatter.2.cloned.1.call-start
  296.5 0.1 select_reduce_fusion
  296.6 6.8 %gather_fusion.1 = bf16[8,8,128,384]{2,3,1,0:T(8,128)(2,1)} fusion(bf16[8,8,128,384]{2,3,1,0:T(8,128)(2,1)} %mini-gather-slice.9, s32[1024]{0:T(1024)S(1)} %pad_clamp_fusion.1), kind=kCustom, calls=%fused_computation.1.clone | custom fusion | bytes 12582944 | tf_op jit(solution)/shard_map/jit(_take)/gather | solution.py:60
  303.4 11.0 %gather_fusion = bf16[8,8,256,384]{2,3,1,0:T(8,128)(2,1)} fusion(bf16[8,8,256,384]{2,3,1,0:T(8,128)(2,1)} %mini-gather-slice.8, s32[1024]{0:T(1024)S(1)} %pad_clamp_fusion.1), kind=kCustom, calls=%fused_computation.clone | custom fusion | bytes 25165856 | tf_op jit(solution)/shard_map/jit(_take)/gather | solution.py:60
  314.4 13.0 %all-to-all-done.3 = bf16[128,24,384]{2,1,0:T(8,128)(2,1)} async-done(((bf16[128,24,384]{2,1,0:T(8,128)(2,1)}), bf16[128,24,384]{2,1,0:T(8,128)(2,1)}, u32[]{:S(2)}, u32[]{:S(2)}) %all-to-all-start.3) | async-done | bytes 2359328 | tf_op jit(solution)/shard_map/all_to_all | solution.py:55
  327.4 2.2 convert_bitcast_fusion
  329.5 2.4 copy.67
  332.0 6.1 %copy.68 = f32[8,384,384]{1,2,0:T(8,128)} copy(f32[8,384,384]{2,1,0:T(8,128)} %bitcast.73) | data formatting | bytes 9437184 | tf_op jit(solution)/shard_map/convert_element_type | solution.py:61
  338.1 18.3 %fusion = f32[8,8,384,256]{2,3,1,0:T(8,128)} fusion(bf16[8,8,128,384]{2,3,1,0:T(8,128)(2,1)} %gather_fusion.1, bf16[8,8,256,384]{2,3,1,0:T(8,128)(2,1)} %gather_fusion, f32[8,384,384]{1,2,0:T(8,128)} %copy.68, pred[8]{0:T(512)(128)(4,1)S(1)} %compare_and_fusion.1, bf16[8,384,256]{2,1,0:T(8,128)(2,1)S(1)} %copy-done), kind=kOutput, calls=%fused_computation.6 | convolution fusion | flops 4907335680 | bytes 50331656 | tf_op jit(solution)/shard_map/ktpq,kqj->ktpj/dot_general | solution.py:64
  356.4 18.9 %fusion.15 = bf16[8,8,256,256]{2,3,1,0:T(8,128)(2,1)} fusion(f32[8,8,384,256]{2,3,1,0:T(8,128)} %fusion, bf16[8,384,256]{2,1,0:T(8,128)(2,1)S(1)} %copy-done), kind=kOutput, calls=%fused_computation.21 | convolution fusion | flops 19335741440 | bytes 35127296 | tf_op jit(solution)/shard_map/kpi,ktpj->ktij/dot_general | solution.py:68
  375.3 0.0 reduce-scatter.2.cloned.1.call-update
  375.3 115.6 %reduce-scatter.2.cloned.1.call-done = bf16[1,8,256,256]{2,3,1,0:T(8,128)(2,1)} async-done(((bf16[8,8,256,256]{2,3,1,0:T(8,128)(2,1)}), bf16[1,8,256,256]{2,3,1,0:T(8,128)(2,1)}) %reduce-scatter.2.cloned.1.call-update) | async-done | bytes 1048592 | tf_op jit(solution)/shard_map/reduce_scatter | solution.py:65
  490.9 2.6 copy.71
  (6 shorter events, 0.0 us)
Async XLA Ops:
  6.5 1.4 copy-start
  155.9 37.2 %copy-start.3 = (bf16[128,128]{1,0:T(8,128)(2,1)S(1)}, bf16[128,128]{1,0:T(8,128)(2,1)}, u32[]{:S(2)}) copy-start(bf16[128,128]{1,0:T(8,128)(2,1)} %param.11) | copy-start | bytes 98308
  195.4 40.3 %copy-start.2 = (bf16[384,384]{1,0:T(8,128)(2,1)S(1)}, bf16[384,384]{1,0:T(8,128)(2,1)}, u32[]{:S(2)}) copy-start(bf16[384,384]{1,0:T(8,128)(2,1)} %param.13) | copy-start | bytes 884740
  234.3 1.4 copy-start.1
  249.6 34.8 %copy-start.4 = (bf16[128,128]{1,0:T(8,128)(2,1)S(1)}, bf16[128,128]{1,0:T(8,128)(2,1)}, u32[]{:S(2)}) copy-start(bf16[128,128]{1,0:T(8,128)(2,1)} %param.12) | copy-start | bytes 98308
  291.2 36.2 %all-to-all-start.3 = ((bf16[128,24,384]{2,1,0:T(8,128)(2,1)}), bf16[128,24,384]{2,1,0:T(8,128)(2,1)}, u32[]{:S(2)}, u32[]{:S(2)}) async-start(bf16[128,24,384]{2,1,0:T(8,128)(2,1)} %copy.66), calls=%async_computation.3 | async-start | bytes 4718592 | tf_op jit(solution)/shard_map/all_to_all | solution.py:55
  296.2 194.7 %reduce-scatter.2.cloned.1.call-start = ((), (), s32[]{:S(2)}) async-start(), calls=%async_computation.5 | async-start | bytes 9437184 | tf_op jit(solution)/shard_map/reduce_scatter | solution.py:65
Sparse Core Ops, SparseCore 0:
  375.4 115.4 reduce-scatter.1
where the time goes:
time: 502 us; the launch traced here: 500 us
  local copies, waits for them, and re-layouts  133 us (26%)
  waiting for transfers between devices  129 us (26%)
  blocking collectives  104 us (21%)
  matrix products  71.2 us (14%)
  other arithmetic  44.7 us (9%)
  between operations  13.5 us (3%)
  starting transfers between devices  5.25 us (1%)
    reduce_scatter x1, waiting for transfers between devices, local(): lax.psum_scatter((scale * jnp.einsum('kpi,ktpj->ktij', colloc.astype(jnp....  116 us
    unnamed x11, local copies, waits for them, and re-layouts  39.6 us
    unnamed x2, other arithmetic  39 us
    all_to_all x1, blocking collectives, local(): lax.all_to_all(polar, 'ta', split_axis=1, concat_axis=0, tiled=True)  36.8 us
    gather x4, local copies, waits for them, and re-layouts, local(): chosen = jnp.take(aux_green, sources, axis=0)  34.5 us
    all_to_all x1, blocking collectives, local(): lax.all_to_all(freq_block, 'ta', split_axis=0, concat_axis=1, tiled=True)  34 us
    all_to_all x1, blocking collectives, local(): lax.all_to_all(screen_freq, 'ta', split_axis=1, concat_axis=0, tiled=True)  33 us
    dot_general x1, matrix products, local(): jnp.einsum('kpi,ktpj->ktij', colloc.astype(jnp.float32), right_prod, prec...  18.9 us
  transfers between devices with their start and end apart: 2, of which 2 were waited for; matrix products, arithmetic and copies ran while one was open for 4% of the time, Pallas kernels for 0%

commit v1 on v0

v1 whole, which is shorter than its diff:
```python
import jax
import jax.numpy as jnp
from jax import lax
from jax.experimental import pallas as pl
from jax.experimental.pallas import tpu as pltpu
from jax.sharding import PartitionSpec as P

MESH = pl.DeviceIdType.MESH
F32, BF16 = jnp.float32, jnp.bfloat16
NK = 8
NT = 8
GROUPS = 3
LANES = 128
MIB = 1 << 20


def dot(a, b, dims=((1,), (0,))):
    return lax.dot_general(a, b, (dims, ((), ())), preferred_element_type=F32)


def project_kernel(kplus_ref, green_ref, colloc_ref, aux_ref, polar_ref, aux_s, mirror_s):
    k = pl.program_id(0)
    p = lax.axis_index("pb")
    rows = jnp.concatenate(
        [colloc_ref[0, pl.ds(pl.multiple_of(128 * g + 16 * p, 16), 16), :] for g in range(GROUPS)], axis=0
    )
    colloc = colloc_ref[0]
    left, right = [], []
    for t in range(NT):
        left.append(dot(rows, green_ref[0, t]).astype(BF16))
        right.append(dot(rows, green_ref[0, t ^ 1], ((1,), (1,))).astype(BF16))
    aux = dot(jnp.concatenate(left, axis=0), colloc, ((1,), (1,))).astype(BF16)
    aux_ref[0] = aux.reshape(NT, 48, 384)
    aux_s[k] = aux.astype(F32).reshape(NT, 48, 384)
    mirror = dot(jnp.concatenate(right, axis=0), colloc, ((1,), (1,))).astype(BF16)
    mirror_s[k] = mirror.astype(F32).reshape(NT, 48, 384)

    @pl.when(k == NK - 1)
    def _():
        def step(i, carry):
            tp, q = i // NK, lax.rem(i, NK)
            for ch in range(GROUPS):
                cols = slice(LANES * ch, LANES * ch + LANES)
                total = None
                for point in range(NK):
                    term = aux_s[kplus_ref[q, point], pl.ds(2 * tp, 2), :, cols] * mirror_s[point, pl.ds(2 * tp, 2), :, cols]
                    total = term if total is None else total + term
                total = (total * (-1.0 / NK)).reshape(2, GROUPS, 2, 8, LANES)
                for g in range(GROUPS):
                    for core in range(2):
                        polar_ref[ch, 2 * q + core, pl.ds(pl.multiple_of(64 * g + 16 * tp, 16), 16), :] = (
                            total[:, g, core].reshape(16, LANES).astype(BF16)
                        )
            return carry

        lax.fori_loop(0, NK * NT // 2, step, 0)


def project(kplus, green, colloc):
    return pl.pallas_call(
        project_kernel,
        grid=(NK,),
        in_specs=[
            pl.BlockSpec(memory_space=pltpu.SMEM),
            pl.BlockSpec((1, NT, 256, 256), lambda k: (k, 0, 0, 0)),
            pl.BlockSpec((1, 384, 256), lambda k: (k, 0, 0)),
        ],
        out_specs=[
            pl.BlockSpec((1, NT, 48, 384), lambda k: (k, 0, 0, 0)),
            pl.BlockSpec((GROUPS, 16, 192, LANES), lambda k: (0, 0, 0, 0)),
        ],
        out_shape=[
            jax.ShapeDtypeStruct((NK, NT, 48, 384), BF16),
            jax.ShapeDtypeStruct((GROUPS, 16, 192, LANES), BF16),
        ],
        scratch_shapes=[pltpu.VMEM((NK, NT, 48, 384), F32), pltpu.VMEM((NK, NT, 48, 384), F32)],
        compiler_params=pltpu.CompilerParams(vmem_limit_bytes=48 * MIB),
        name="project",
    )(kplus, green, colloc)


def spread(table, wide_ref):
    row = lax.broadcasted_iota(jnp.int32, (1024, 128), 0) // 8
    pick = (row == lax.broadcasted_iota(jnp.int32, (1024, 128), 1)).astype(BF16)
    across = dot(table, pick, ((1,), (1,))).astype(BF16)
    for part in range(4):
        full = dot(pick[256 * part : 256 * part + 256], across)
        same = lax.broadcasted_iota(jnp.int32, (256, 1024), 0) % 8 == lax.broadcasted_iota(jnp.int32, (256, 1024), 1) % 8
        wide_ref[256 * part : 256 * part + 256, :] = jnp.where(same, full, 0.0).astype(BF16)


def transform(wide_ref, src, dst, ch):
    x = jnp.concatenate([src[ch, :, 64 * g : 64 * g + 64, :].reshape(1024, LANES) for g in range(GROUPS)], axis=1)
    for part in range(4):
        y = dot(wide_ref[256 * part : 256 * part + 256, :], x).astype(BF16)
        for g in range(GROUPS):
            dst[ch, 4 * part : 4 * part + 4, 64 * g : 64 * g + 64, :] = y[:, LANES * g : LANES * g + LANES].reshape(4, 64, LANES)


def screen_kernel(
    polar_ref, freq_ref, time_ref, coul_ref, out_ref,
    times, freqs, whole, chain, back, stamps, wide, send_sem, recv_sem, own_sem,
):
    pb, ta = lax.axis_index("pb"), lax.axis_index("ta")
    z_hi, z_lo, y, core = pb // 4, ta // 8, lax.rem(ta // 2, 4), lax.rem(ta, 2)
    own_q = y + 4 * lax.bitwise_xor(z_lo, z_hi)
    own_block = 2 * pb + core

    def line(j):
        return (pb, j)

    def plane(j):
        other = j // 2
        other_lo = lax.bitwise_xor(lax.bitwise_xor(z_lo, z_hi), other // 4)
        return (other, 8 * other_lo + 2 * y + lax.rem(j, 2))

    def transfer_slot(j):
        return 2 * (lax.rem(j // 2, 4) + 4 * lax.bitwise_xor(j // 8, z_hi)) + lax.rem(j, 2)

    same = lambda j: j
    stages = (
        (polar_ref, transfer_slot, times, ta, line, ta),
        (freqs, same, whole, own_block, plane, own_block),
        (chain, same, back, own_block, plane, own_block),
        (stamps, same, out_ref, 2 * own_q + core, line, ta),
    )

    def send(stage, ch):
        src, slot, dst, there, device, me = stages[stage]

        def go(s, carry):
            j = lax.bitwise_xor(me, s)
            pltpu.make_async_remote_copy(
                src_ref=src.at[ch, slot(j)],
                dst_ref=dst.at[ch, there],
                send_sem=send_sem.at[stage, ch],
                recv_sem=recv_sem.at[stage, ch],
                device_id=device(j),
                device_id_type=MESH,
            ).start()
            return carry

        lax.fori_loop(1, 16, go, 0)
        pltpu.make_async_copy(src.at[ch, slot(me)], dst.at[ch, there], own_sem.at[stage, ch]).start()

    def receive(stage, ch):
        src, slot, dst, there, device, me = stages[stage]
        part = dst.at[ch, pl.ds(0, 15)]
        pltpu.make_async_copy(part, part, recv_sem.at[stage, ch]).wait()
        pltpu.make_async_copy(src.at[ch, slot(me)], dst.at[ch, there], own_sem.at[stage, ch]).wait()

    def sent(stage, ch):
        part = stages[stage][0].at[ch, pl.ds(0, 15)]
        pltpu.make_async_copy(part, part, send_sem.at[stage, ch]).wait()

    barrier = pltpu.get_barrier_semaphore()

    def greet(s, carry):
        pl.semaphore_signal(barrier, inc=1, device_id=line(lax.bitwise_xor(ta, s)), device_id_type=MESH)
        pl.semaphore_signal(barrier, inc=1, device_id=plane(lax.bitwise_xor(own_block, s)), device_id_type=MESH)
        return carry

    lax.fori_loop(1, 16, greet, 0)
    pl.semaphore_wait(barrier, 30)

    send(0, 0)
    send(0, 1)
    spread(freq_ref[...], wide)
    for ch in range(GROUPS):
        receive(0, ch)
        if ch == 0:
            send(0, 2)
        transform(wide, times, freqs, ch)
        send(1, ch)
    spread(time_ref[...], wide)
    for ch in range(GROUPS):
        receive(1, ch)

    def pair(wp, carry):
        coul = coul_ref[...]
        lines = [
            [
                whole[ch, :, pl.ds(pl.multiple_of(64 * g + 16 * wp, 16), 16), :].astype(F32).reshape(16, 2, 8, LANES)
                for g in range(GROUPS)
            ]
            for ch in range(GROUPS)
        ]
        screened = []
        for j in range(2):
            polar = jnp.concatenate(
                [jnp.concatenate([lines[ch][g][:, j].reshape(128, LANES) for g in range(GROUPS)], axis=0) for ch in range(GROUPS)],
                axis=1,
            )
            low = polar.astype(BF16)
            first = dot(low, coul).astype(BF16)
            series = (polar + dot(first, low)).astype(BF16)
            left = dot(coul, series).astype(BF16)
            screened.append(dot(left, coul))
        for ch in range(GROUPS):
            for g in range(GROUPS):
                both = [
                    s[128 * g : 128 * g + 128, LANES * ch : LANES * ch + LANES].reshape(16, 1, 8, LANES) for s in screened
                ]
                chain[ch, :, pl.ds(pl.multiple_of(64 * g + 16 * wp, 16), 16), :] = (
                    jnp.concatenate(both, axis=1).reshape(16, 16, LANES).astype(BF16)
                )
        return carry

    lax.fori_loop(0, NT // 2, pair, 0)
    send(2, 0)
    send(2, 1)
    for ch in range(GROUPS):
        receive(2, ch)
        if ch == 0:
            send(2, 2)
        transform(wide, back, stamps, ch)
        send(3, ch)
    for ch in range(GROUPS):
        receive(3, ch)
    for stage in range(4):
        for ch in range(GROUPS):
            sent(stage, ch)


def screen(polar, to_freq, to_time, coulomb):
    block = (GROUPS, 16, 192, LANES)
    vmem = pl.BlockSpec(memory_space=pltpu.VMEM)
    hbm = pl.BlockSpec(memory_space=pl.ANY)
    return pl.pallas_call(
        screen_kernel,
        in_specs=[hbm, vmem, vmem, vmem],
        out_specs=hbm,
        out_shape=jax.ShapeDtypeStruct(block, BF16),
        scratch_shapes=[pltpu.VMEM(block, BF16)] * 6
        + [pltpu.VMEM((1024, 1024), BF16)]
        + [pltpu.SemaphoreType.DMA((4, GROUPS))] * 3,
        compiler_params=pltpu.CompilerParams(collective_id=0, has_side_effects=True, vmem_limit_bytes=48 * MIB),
        name="screen",
    )(polar, to_freq, to_time, coulomb)


def hadamard_kernel(source_ref, aux_ref, screen_ref, colloc_ref, out_ref, screen_s, sum_s):
    def step(tp, carry):
        for q in range(NK):
            for ch in range(GROUPS):
                for g in range(GROUPS):
                    for core in range(2):
                        part = screen_ref[ch, 2 * q + core, pl.ds(pl.multiple_of(64 * g + 16 * tp, 16), 16), :].astype(F32)
                        screen_s[q, :, 16 * g + 8 * core : 16 * g + 8 * core + 8, LANES * ch : LANES * ch + LANES] = (
                            part.reshape(2, 8, LANES)
                        )

        def target(c, inner):
            for ch in range(GROUPS):
                cols = slice(LANES * ch, LANES * ch + LANES)
                total = None
                for q in range(NK):
                    term = aux_ref[source_ref[q, c], pl.ds(2 * tp, 2), :, cols].astype(F32) * screen_s[q, :, :, cols]
                    total = term if total is None else total + term
                sum_s[c, pl.ds(pl.multiple_of(96 * tp, 32), 96), cols] = total.astype(BF16).reshape(96, LANES)
            return inner

        lax.fori_loop(0, NK, target, 0)
        return carry

    lax.fori_loop(0, NT // 2, step, 0)

    def project_out(c, carry):
        out_ref[c] = dot(sum_s[c], colloc_ref[c]).astype(BF16).reshape(NT, GROUPS, 16, 256)
        return carry

    lax.fori_loop(0, NK, project_out, 0)


def hadamard(sources, aux, screened, colloc):
    vmem = pl.BlockSpec(memory_space=pltpu.VMEM)
    return pl.pallas_call(
        hadamard_kernel,
        in_specs=[pl.BlockSpec(memory_space=pltpu.SMEM), vmem, vmem, vmem],
        out_specs=vmem,
        out_shape=jax.ShapeDtypeStruct((NK, NT, GROUPS, 16, 256), BF16),
        scratch_shapes=[pltpu.VMEM((NK, 2, 48, 384), F32), pltpu.VMEM((NK, NT * 48, 384), BF16)],
        compiler_params=pltpu.CompilerParams(vmem_limit_bytes=48 * MIB),
        name="hadamard",
    )(sources, aux, screened, colloc)


def exchange_kernel(src, dst, send_sem, recv_sem, own_sem):
    pb, ta = lax.axis_index("pb"), lax.axis_index("ta")
    barrier = pltpu.get_barrier_semaphore()

    def greet(s, carry):
        pl.semaphore_signal(barrier, inc=1, device_id=(lax.bitwise_xor(pb, s), ta), device_id_type=MESH)
        return carry

    lax.fori_loop(1, NK, greet, 0)
    pl.semaphore_wait(barrier, NK - 1)

    def go(s, carry):
        j = lax.bitwise_xor(pb, s)
        pltpu.make_async_remote_copy(
            src_ref=src.at[j],
            dst_ref=dst.at[pb],
            send_sem=send_sem,
            recv_sem=recv_sem,
            device_id=(j, ta),
            device_id_type=MESH,
        ).start()
        return carry

    lax.fori_loop(1, NK, go, 0)
    own = pltpu.make_async_copy(src.at[pb], dst.at[pb], own_sem)
    own.start()
    own.wait()
    part = dst.at[pl.ds(0, NK - 1)]
    pltpu.make_async_copy(part, part, send_sem).wait()
    pltpu.make_async_copy(part, part, recv_sem).wait()


def exchange(right):
    hbm = pl.BlockSpec(memory_space=pl.ANY)
    return pl.pallas_call(
        exchange_kernel,
        in_specs=[hbm],
        out_specs=hbm,
        out_shape=jax.ShapeDtypeStruct(right.shape, BF16),
        scratch_shapes=[pltpu.SemaphoreType.DMA] * 3,
        compiler_params=pltpu.CompilerParams(collective_id=1, has_side_effects=True),
        name="exchange",
    )(right)


def sigma_kernel(place_ref, right_ref, colloc_ref, out_ref):
    right = right_ref[...].reshape(NK, GROUPS, 16, 256)
    whole = jnp.concatenate([right[:, g].reshape(128, 256) for g in range(GROUPS)], axis=0)
    out_ref[0, 0] = dot(colloc_ref[0], whole, ((0,), (0,))) * (-1.0 / NK)


def outer(right, colloc, place):
    return pl.pallas_call(
        sigma_kernel,
        grid_spec=pltpu.PrefetchScalarGridSpec(
            num_scalar_prefetch=1,
            grid=(NT,),
            in_specs=[
                pl.BlockSpec((NK, 1, GROUPS, 16, 256), lambda t, place: (0, t, 0, 0, 0)),
                pl.BlockSpec((1, 384, 256), lambda t, place: (place[0], 0, 0)),
            ],
            out_specs=pl.BlockSpec((1, 1, 256, 256), lambda t, place: (0, t, 0, 0)),
        ),
        out_shape=jax.ShapeDtypeStruct((1, NT, 256, 256), F32),
        name="sigma",
    )(place, right, colloc)


def local(green, colloc, kplus, to_freq, to_time, coulomb):
    points = jnp.arange(NK, dtype=jnp.int32)
    sources = jnp.sum(jnp.where(kplus[:, :, None] == points[None, None, :], points[None, :, None], 0), axis=1)
    aux, polar = project(kplus, green, colloc)
    screened = screen(polar, to_freq, to_time, coulomb)
    right = exchange(hadamard(sources, aux, screened, colloc))
    return outer(right, colloc, lax.axis_index("pb").astype(jnp.int32).reshape(1))


def solution(mesh):
    in_specs = (P(None, "ta", None, None), P(), P(), P(), P(), P())
    out_specs = P("pb", "ta", None, None)
    return jax.shard_map(local, mesh=mesh, in_specs=in_specs, out_specs=out_specs, check_vma=False)
```

time: 502 us -> 169 us (0.34)
  Pallas kernels: 0 us -> 162 us
  waiting for transfers between devices: 129 us -> 0 us
  local copies, waits for them, and re-layouts: 133 us -> 6.32 us
  blocking collectives: 104 us -> 0 us
  matrix products: 71.2 us -> 0 us
  other arithmetic: 44.7 us -> 0.09 us
  between operations: 13.5 us -> 0.08 us
  starting transfers between devices: 5.25 us -> 0 us
    pallas_call x0 -> x5, Pallas kernels: none -> 162 us  [the longest x1 106 us: screen(): pl.pallas_call(screen_kernel, in_specs=[hbm, vmem, vmem, vmem], out_specs...]
    reduce_scatter x1 -> x0, waiting for transfers between devices: 116 us -> none  [local(): lax.psum_scatter((scale * jnp.einsum('kpi,ktpj->ktij', colloc.astype(jnp....]
    all_to_all x3 -> x0, blocking collectives: 104 us -> none  [the longest x1 36.8 us: local(): lax.all_to_all(polar, 'ta', split_axis=1, concat_axis=0, tiled=True)]
    dot_general x8 -> x0, matrix products: 71.2 us -> none  [the longest x1 18.9 us: local(): jnp.einsum('kpi,ktpj->ktij', colloc.astype(jnp.float32), right_prod, prec...]
    gather x6 -> x0, local copies, waits for them, and re-layouts: 52.1 us -> none  [the longest x4 34.5 us: local(): chosen = jnp.take(aux_green, sources, axis=0)]
    unnamed x2 -> x0, other arithmetic: 39 us -> none
    unnamed x11 -> x20, local copies, waits for them, and re-layouts: 39.6 us -> 6.32 us
    convert_element_type x6 -> x0, local copies, waits for them, and re-layouts: 21.6 us -> none  [the longest x2 8.57 us: local(): screen_time[None].astype(jnp.float32)]
  transfers between devices with their start and end apart: 2 -> 0, of which waited for: 2 -> 0; matrix products, arithmetic and copies ran while one was open for 4% -> 0% of each run, Pallas kernels for 0% -> 0%
where the time goes in v1:
time: 169 us; the launch traced here: 168 us
  Pallas kernels  162 us (96%)
  local copies, waits for them, and re-layouts  6.32 us (4%)
    pallas_call x1, Pallas kernels, screen(): pl.pallas_call(screen_kernel, in_specs=[hbm, vmem, vmem, vmem], out_specs...  106 us
    pallas_call x1, Pallas kernels, exchange(): pl.pallas_call(exchange_kernel, in_specs=[hbm], out_specs=hbm, out_shape=...  25.3 us
    pallas_call x1, Pallas kernels, project(): pl.pallas_call(project_kernel, grid=(NK,), in_specs=[pl.BlockSpec(memory_...  14.8 us
    pallas_call x1, Pallas kernels, hadamard(): pl.pallas_call(hadamard_kernel, in_specs=[pl.BlockSpec(memory_space=pltpu...  8.51 us
    pallas_call x1, Pallas kernels, outer(): pl.pallas_call(sigma_kernel, grid_spec=pltpu.PrefetchScalarGridSpec(num_s...  6.58 us
    unnamed x20, local copies, waits for them, and re-layouts  6.32 us

profile of v1, /device:TPU:1, one launch (start us, length us, event | category | flops | bytes accessed | tf_op | source)
XLA Modules:
  0.0 168.1 jit_solution(13910347917073962436)
XLA Ops:
  0.0 0.0 copy-start
  0.0 1.4 copy-done
  1.4 0.0 copy-start.8
  1.4 0.7 copy-done.8
  2.1 0.0 copy-start.5
  2.1 0.0 copy-start.6
  2.1 0.0 copy-start.7
  2.1 14.8 %project.1 = (bf16[8,8,48,384]{3,2,1,0:T(8,128)(2,1)S(1)}, bf16[3,16,192,128]{3,2,1,0:T(8,128)(2,1)}) custom-call(s32[8,8]{1,0:T(8,128)S(1)} %copy-done.8, bf16[8,8,256,256]{3,2,1,0:T(8,128)(2,1)} %green_ref.1, bf16[8,384,256]{2,1,0:T(8,128)(2,1)S(1)} %copy-done), custom_call_target="tpu_custom_call" | custom-call | tf_op jit(solution)/shard_map/project/pallas_call | solution.py:60
  16.9 0.0 copy-done.5
  16.9 0.0 copy-done.6
  16.9 0.0 copy-done.7
  16.9 0.0 copy-start.4
  17.0 1.7 copy-done.4
  18.6 0.0 copy-start.9
  18.6 0.0 copy-start.1
  18.6 106.4 %screen.1.screen_ref = bf16[3,16,192,128]{3,2,1,0:T(8,128)(2,1)S(1)} custom-call(bf16[3,16,192,128]{3,2,1,0:T(8,128)(2,1)S(1)} %copy-done.4, bf16[128,128]{1,0:T(8,128)(2,1)S(1)} %copy-done.6, bf16[128,128]{1,0:T(8,128)(2,1)S(1)} %copy-done.7, bf16[384,384]{1,0:T(8,128)(2,1)S(1)} %copy-done.5), custom_call_target="tpu_custom_call" | custom-call | tf_op jit(solution)/shard_map/screen/pallas_call | solution.py:229
  125.0 0.0 copy-start.2
  125.0 1.4 copy-done.2
  126.4 0.0 copy-done.9
  126.4 0.1 select_reduce_fusion.source_ref
  126.5 0.0 copy-done.1
  126.5 8.5 %hadamard.1.src = bf16[8,8,3,16,256]{4,3,2,1,0:T(8,128)(2,1)S(1)} custom-call(s32[8,8]{1,0:T(8,128)S(1)} %select_reduce_fusion.source_ref, bf16[8,8,48,384]{3,2,1,0:T(8,128)(2,1)S(1)} %get-tuple-element.7.aux_ref, bf16[3,16,192,128]{3,2,1,0:T(8,128)(2,1)} %copy-done.2, bf16[8,384,256]{2,1,0:T(8,128)(2,1)S(1)} %copy-done.1), custom_call_target="tpu_custom_call" | custom-call | tf_op jit(solution)/shard_map/hadamard/pallas_call | solution.py:277
  135.1 0.0 copy-start.3
  135.1 1.1 copy-done.3
  136.2 25.3 %exchange.1.right_ref = bf16[8,8,3,16,256]{4,3,2,1,0:T(8,128)(2,1)} custom-call(bf16[8,8,3,16,256]{4,3,2,1,0:T(8,128)(2,1)} %copy-done.3), custom_call_target="tpu_custom_call" | custom-call | tf_op jit(solution)/shard_map/exchange/pallas_call | solution.py:322
  161.5 6.6 %sigma.1 = f32[1,8,256,256]{3,2,1,0:T(8,128)} custom-call(s32[1]{0:T(128)} %bitcast.place_ref, bf16[8,8,3,16,256]{4,3,2,1,0:T(8,128)(2,1)} %exchange.1.right_ref, bf16[8,384,256]{2,1,0:T(8,128)(2,1)} %colloc_ref.5), custom_call_target="tpu_custom_call" | custom-call | tf_op jit(solution)/shard_map/sigma/pallas_call | solution.py:340
Async XLA Ops:
  0.0 1.4 copy-start
  1.4 0.7 copy-start.8
  2.1 14.8 %copy-start.5 = (bf16[384,384]{1,0:T(8,128)(2,1)S(1)}, bf16[384,384]{1,0:T(8,128)(2,1)}, u32[]{:S(2)}) copy-start(bf16[384,384]{1,0:T(8,128)(2,1)} %coul_ref.1) | copy-start | bytes 884740
  2.1 14.8 %copy-start.6 = (bf16[128,128]{1,0:T(8,128)(2,1)S(1)}, bf16[128,128]{1,0:T(8,128)(2,1)}, u32[]{:S(2)}) copy-start(bf16[128,128]{1,0:T(8,128)(2,1)} %freq_ref.1) | copy-start | bytes 98308
  2.1 14.8 %copy-start.7 = (bf16[128,128]{1,0:T(8,128)(2,1)S(1)}, bf16[128,128]{1,0:T(8,128)(2,1)}, u32[]{:S(2)}) copy-start(bf16[128,128]{1,0:T(8,128)(2,1)} %time_ref.1) | copy-start | bytes 98308
  16.9 1.7 copy-start.4
  18.6 107.8 %copy-start.9 = (s32[8,8]{1,0:T(8,128)S(1)}, s32[8,8]{1,0:T(8,128)}, u32[]{:S(2)}) copy-start(s32[8,8]{1,0:T(8,128)} %kplus_ref.1) | copy-start | bytes 772
  18.6 107.9 %copy-start.1 = (bf16[8,384,256]{2,1,0:T(8,128)(2,1)S(1)}, bf16[8,384,256]{2,1,0:T(8,128)(2,1)}, u32[]{:S(2)}) copy-start(bf16[8,384,256]{2,1,0:T(8,128)(2,1)} %colloc_ref.5) | copy-start | bytes 4718596
  125.0 1.4 copy-start.2
  135.1 1.1 copy-start.3

commit v2 on v0

v2 whole, which is shorter than its diff:
```python
import jax
import jax.numpy as jnp
from jax import lax
from jax.experimental import pallas as pl
from jax.experimental.pallas import tpu as pltpu
from jax.sharding import PartitionSpec as P

MESH = pl.DeviceIdType.MESH
F32, BF16 = jnp.float32, jnp.bfloat16
NK = 8
NT = 8
GROUPS = 3
PARTS = GROUPS * GROUPS
LANES = 128
MIB = 1 << 20


def dot(a, b, dims=((1,), (0,))):
    return lax.dot_general(a, b, (dims, ((), ())), preferred_element_type=F32)


def spread(table, wide_ref):
    row = lax.broadcasted_iota(jnp.int32, (1024, 128), 0) // 8
    pick = (row == lax.broadcasted_iota(jnp.int32, (1024, 128), 1)).astype(BF16)
    across = dot(table, pick, ((1,), (1,))).astype(BF16)
    for part in range(4):
        full = dot(pick[256 * part : 256 * part + 256], across)
        same = lax.broadcasted_iota(jnp.int32, (256, 1024), 0) % 8 == lax.broadcasted_iota(jnp.int32, (256, 1024), 1) % 8
        wide_ref[256 * part : 256 * part + 256, :] = jnp.where(same, full, 0.0).astype(BF16)


def transform(wide_ref, src, dst, n):
    x = src[n].reshape(1024, LANES)
    for part in range(4):
        y = dot(wide_ref[256 * part : 256 * part + 256, :], x)
        dst[n, 4 * part : 4 * part + 4] = y.astype(BF16).reshape(4, 64, LANES)


def step_kernel(
    kplus_ref, source_ref, green_ref, colloc_ref, freq_ref, time_ref, coul_ref, out_ref,
    green_s, colloc_s, left_s, right_s, aux_s, mirror_s, polar, times, freqs, whole, chain, back, stamps, screen, wide,
    sum_s, half_s, load_sem, send_sem, recv_sem, own_sem, last_send, last_recv, last_own,
):
    pb, ta = lax.axis_index("pb"), lax.axis_index("ta")
    z_hi, z_lo, y, core = pb // 4, ta // 8, lax.rem(ta // 2, 4), lax.rem(ta, 2)
    own_q = y + 4 * lax.bitwise_xor(z_lo, z_hi)
    own_block = 2 * pb + core

    def load(k):
        return pltpu.make_async_copy(green_ref.at[k], green_s.at[k], load_sem.at[k])

    load_colloc = pltpu.make_async_copy(colloc_ref, colloc_s, load_sem.at[NK])
    load_colloc.start()
    for k in range(NK):
        load(k).start()

    def line(j):
        return (pb, j)

    def plane(j):
        other = j // 2
        other_lo = lax.bitwise_xor(lax.bitwise_xor(z_lo, z_hi), other // 4)
        return (other, 8 * other_lo + 2 * y + lax.rem(j, 2))

    def transfer_slot(j):
        return 2 * (lax.rem(j // 2, 4) + 4 * lax.bitwise_xor(j // 8, z_hi)) + lax.rem(j, 2)

    same = lambda j: j
    stages = (
        (polar, transfer_slot, times, ta, line, ta),
        (freqs, same, whole, own_block, plane, own_block),
        (chain, same, back, own_block, plane, own_block),
        (stamps, same, screen, 2 * own_q + core, line, ta),
    )

    def send(stage, n, first=0, size=64):
        src, slot, dst, there, device, me = stages[stage]
        rows = pl.ds(first, size)

        def go(s, carry):
            j = lax.bitwise_xor(me, s)
            pltpu.make_async_remote_copy(
                src_ref=src.at[n, slot(j), rows],
                dst_ref=dst.at[n, there, rows],
                send_sem=send_sem.at[stage, n],
                recv_sem=recv_sem.at[stage, n],
                device_id=device(j),
                device_id_type=MESH,
            ).start()
            return carry

        lax.fori_loop(1, 16, go, 0)
        pltpu.make_async_copy(src.at[n, slot(me), rows], dst.at[n, there, rows], own_sem.at[stage, n]).start()

    def receive(stage, n):
        src, slot, dst, there, device, me = stages[stage]
        part = dst.at[n, pl.ds(0, 15)]
        pltpu.make_async_copy(part, part, recv_sem.at[stage, n]).wait()
        pltpu.make_async_copy(src.at[n, slot(me)], dst.at[n, there], own_sem.at[stage, n]).wait()

    def sent(stage, n):
        part = stages[stage][0].at[n, pl.ds(0, 15)]
        pltpu.make_async_copy(part, part, send_sem.at[stage, n]).wait()

    barrier = pltpu.get_barrier_semaphore()

    def greet(s, carry):
        pl.semaphore_signal(barrier, inc=1, device_id=line(lax.bitwise_xor(ta, s)), device_id_type=MESH)
        pl.semaphore_signal(barrier, inc=1, device_id=plane(lax.bitwise_xor(own_block, s)), device_id_type=MESH)
        return carry

    def greet_last(s, carry):
        pl.semaphore_signal(barrier, inc=1, device_id=(lax.bitwise_xor(pb, s), ta), device_id_type=MESH)
        return carry

    lax.fori_loop(1, 16, greet, 0)
    lax.fori_loop(1, NK, greet_last, 0)

    load_colloc.wait()

    def project(k, carry):
        load(k).wait()
        rows = jnp.concatenate(
            [colloc_s[k, pl.ds(pl.multiple_of(128 * g + 16 * pb, 16), 16), :] for g in range(GROUPS)], axis=0
        )
        left = [dot(rows, green_s[k, t]).reshape(6, 1, 8, 256) for t in range(NT)]
        right = [dot(rows, green_s[k, t ^ 1], ((1,), (1,))).reshape(6, 1, 8, 256) for t in range(NT)]
        left_s[k] = jnp.concatenate(left, axis=1).reshape(384, 256).astype(BF16)
        right_s[k] = jnp.concatenate(right, axis=1).reshape(384, 256).astype(BF16)
        return carry

    lax.fori_loop(0, NK, project, 0)
    pl.semaphore_wait(barrier, 30 + NK - 1)

    for ch in range(GROUPS):

        def widen(k, carry):
            columns = colloc_s[k, LANES * ch : LANES * ch + LANES, :]
            aux = dot(left_s[k], columns, ((1,), (1,)))
            mirror = dot(right_s[k], columns, ((1,), (1,)))
            for g in range(GROUPS):
                aux_s[3 * ch + g, k] = aux[128 * g : 128 * g + 128]
                mirror_s[g, k] = mirror[128 * g : 128 * g + 128]
            return carry

        lax.fori_loop(0, NK, widen, 0)
        for g in range(GROUPS):
            n = 3 * ch + g

            def polarize(i, carry):
                rows = pl.ds(pl.multiple_of(32 * i, 32), 32)
                mirrors = [mirror_s[g, k, rows, :] for k in range(NK)]
                for q in range(NK):
                    total = None
                    for k in range(NK):
                        term = aux_s[n, kplus_ref[q, k], rows, :] * mirrors[k]
                        total = term if total is None else total + term
                    polar[n, 2 * q + i // 2, pl.ds(pl.multiple_of(32 * lax.rem(i, 2), 32), 32), :] = (
                        total * (-1.0 / NK)
                    ).astype(BF16)
                return carry

            lax.fori_loop(0, 4, polarize, 0)
            send(0, n)

    spread(freq_ref[...], wide)
    for n in range(PARTS):
        receive(0, n)
        transform(wide, times, freqs, n)
        send(1, n)
    spread(time_ref[...], wide)
    for n in range(PARTS):
        receive(1, n)

    def pair(wp, carry):
        coul = coul_ref[...]
        rows = pl.ds(pl.multiple_of(16 * wp, 16), 16)
        lines = [whole[n, :, rows, :].astype(F32).reshape(16, 2, 8, LANES) for n in range(PARTS)]
        screened = []
        for j in range(2):
            full = jnp.concatenate(
                [
                    jnp.concatenate([lines[3 * ch + g][:, j].reshape(128, LANES) for g in range(GROUPS)], axis=0)
                    for ch in range(GROUPS)
                ],
                axis=1,
            )
            low = full.astype(BF16)
            first = dot(low, coul).astype(BF16)
            series = (full + dot(first, low)).astype(BF16)
            left = dot(coul, series).astype(BF16)
            screened.append(dot(left, coul))
        for ch in range(GROUPS):
            for g in range(GROUPS):
                both = [
                    s[128 * g : 128 * g + 128, LANES * ch : LANES * ch + LANES].reshape(16, 1, 8, LANES) for s in screened
                ]
                chain[3 * ch + g, :, rows, :] = jnp.concatenate(both, axis=1).reshape(16, 16, LANES).astype(BF16)
        return carry

    order = [3 * ch + g for g in range(GROUPS) for ch in range(GROUPS)]
    ahead = 3
    lax.fori_loop(0, 2, pair, 0)
    for n in order[:ahead]:
        send(2, n, 0, 32)
    lax.fori_loop(2, 4, pair, 0)
    for at, n in enumerate(order):
        send(2, n, 32, 32)
        if at + ahead < PARTS:
            send(2, order[at + ahead], 0, 32)

    last = []
    for at, n in enumerate(order):
        receive(2, n)
        transform(wide, back, stamps, n)
        send(3, n)
    for g in range(GROUPS):
        for ch in range(GROUPS):
            n = 3 * ch + g
            receive(3, n)

            def weigh(i, carry):
                rows = pl.ds(pl.multiple_of(32 * i, 32), 32)
                here = pl.ds(pl.multiple_of(32 * lax.rem(i, 2), 32), 32)
                screens = [screen[n, 2 * q + i // 2, here, :].astype(F32) for q in range(NK)]
                for c in range(NK):
                    total = None
                    for q in range(NK):
                        term = aux_s[n, source_ref[q, c], rows, :] * screens[q]
                        total = term if total is None else total + term
                    sum_s[c, rows, LANES * ch : LANES * ch + LANES] = total.astype(BF16)
                return carry

            lax.fori_loop(0, 4, weigh, 0)

        def halve(s, carry):
            c = lax.bitwise_xor(pb, s)
            half_s[g, c] = dot(sum_s[c], colloc_s[c]).astype(BF16)

            @pl.when(s > 0)
            def _():
                pltpu.make_async_remote_copy(
                    src_ref=half_s.at[g, c],
                    dst_ref=out_ref.at[g, pb],
                    send_sem=last_send.at[g],
                    recv_sem=last_recv.at[g],
                    device_id=(c, ta),
                    device_id_type=MESH,
                ).start()

            return carry

        lax.fori_loop(0, NK, halve, 0)
        own = pltpu.make_async_copy(half_s.at[g, pb], out_ref.at[g, pb], last_own.at[g])
        own.start()
        last.append(own)
    for g in range(GROUPS):
        last[g].wait()
        part = out_ref.at[g, pl.ds(0, NK - 1)]
        pltpu.make_async_copy(part, part, last_recv.at[g]).wait()
        part = half_s.at[g, pl.ds(0, NK - 1)]
        pltpu.make_async_copy(part, part, last_send.at[g]).wait()
    for stage in range(4):
        for n in range(PARTS):
            sent(stage, n)


def step(kplus, sources, green, colloc, to_freq, to_time, coulomb):
    block = (PARTS, 16, 64, LANES)
    vmem = pl.BlockSpec(memory_space=pltpu.VMEM)
    smem = pl.BlockSpec(memory_space=pltpu.SMEM)
    hbm = pl.BlockSpec(memory_space=pl.ANY)
    dma = pltpu.SemaphoreType.DMA
    return pl.pallas_call(
        step_kernel,
        in_specs=[smem, smem, hbm, hbm, vmem, vmem, vmem],
        out_specs=hbm,
        out_shape=jax.ShapeDtypeStruct((GROUPS, NK, 128, 256), BF16),
        scratch_shapes=[
            pltpu.VMEM((NK, NT, 256, 256), BF16),
            pltpu.VMEM((NK, 384, 256), BF16),
            pltpu.VMEM((NK, 384, 256), BF16),
            pltpu.VMEM((NK, 384, 256), BF16),
            pltpu.VMEM((PARTS, NK, 128, LANES), F32),
            pltpu.VMEM((GROUPS, NK, 128, LANES), F32),
        ]
        + [pltpu.VMEM(block, BF16)] * 8
        + [
            pltpu.VMEM((1024, 1024), BF16),
            pltpu.VMEM((NK, 128, 384), BF16),
            pltpu.VMEM((GROUPS, NK, 128, 256), BF16),
            dma((NK + 1,)),
            dma((4, PARTS)),
            dma((4, PARTS)),
            dma((4, PARTS)),
            dma((GROUPS,)),
            dma((GROUPS,)),
            dma((GROUPS,)),
        ],
        compiler_params=pltpu.CompilerParams(collective_id=0, has_side_effects=True, vmem_limit_bytes=56 * MIB),
        name="step",
    )(kplus, sources, green, colloc, to_freq, to_time, coulomb)


def sigma_kernel(place_ref, half_ref, colloc_ref, out_ref):
    half = half_ref[...].astype(F32).reshape(GROUPS, NK, 2, 2, 8, 256)
    for j in range(2):
        whole = half[:, :, :, j].reshape(384, 256).astype(BF16)
        out_ref[0, j] = dot(colloc_ref[0], whole, ((0,), (0,))) * (-1.0 / NK)


def sigma(half, colloc, place):
    return pl.pallas_call(
        sigma_kernel,
        grid_spec=pltpu.PrefetchScalarGridSpec(
            num_scalar_prefetch=1,
            grid=(NT // 2,),
            in_specs=[
                pl.BlockSpec((GROUPS, NK, 2, 16, 256), lambda tp, place: (0, 0, 0, tp, 0)),
                pl.BlockSpec((1, 384, 256), lambda tp, place: (place[0], 0, 0)),
            ],
            out_specs=pl.BlockSpec((1, 2, 256, 256), lambda tp, place: (0, tp, 0, 0)),
        ),
        out_shape=jax.ShapeDtypeStruct((1, NT, 256, 256), F32),
        name="sigma",
    )(place, half.reshape(GROUPS, NK, 2, 64, 256), colloc)


def local(green, colloc, kplus, to_freq, to_time, coulomb):
    points = jnp.arange(NK, dtype=jnp.int32)
    sources = jnp.sum(jnp.where(kplus[:, :, None] == points[None, None, :], points[None, :, None], 0), axis=1)
    half = step(kplus, sources, green, colloc, to_freq, to_time, coulomb)
    return sigma(half, colloc, lax.axis_index("pb").astype(jnp.int32).reshape(1))


def solution(mesh):
    in_specs = (P(None, "ta", None, None), P(), P(), P(), P(), P())
    out_specs = P("pb", "ta", None, None)
    return jax.shard_map(local, mesh=mesh, in_specs=in_specs, out_specs=out_specs, check_vma=False)
```

time: 502 us -> 126 us (0.25)
  local copies, waits for them, and re-layouts: 133 us -> 0 us
  waiting for transfers between devices: 129 us -> 0 us
  Pallas kernels: 0 us -> 125 us
  blocking collectives: 104 us -> 0 us
  matrix products: 71.2 us -> 0 us
  other arithmetic: 44.7 us -> 1.36 us
  between operations: 13.5 us -> 0.01 us
  starting transfers between devices: 5.25 us -> 0 us
    pallas_call x0 -> x2, Pallas kernels: none -> 125 us  [the longest x1 120 us: step(): pl.pallas_call(step_kernel, in_specs=[smem, smem, hbm, hbm, vmem, vmem, v...]
    reduce_scatter x1 -> x0, waiting for transfers between devices: 116 us -> none  [local(): lax.psum_scatter((scale * jnp.einsum('kpi,ktpj->ktij', colloc.astype(jnp....]
    all_to_all x3 -> x0, blocking collectives: 104 us -> none  [the longest x1 36.8 us: local(): lax.all_to_all(polar, 'ta', split_axis=1, concat_axis=0, tiled=True)]
    dot_general x8 -> x0, matrix products: 71.2 us -> none  [the longest x1 18.9 us: local(): jnp.einsum('kpi,ktpj->ktij', colloc.astype(jnp.float32), right_prod, prec...]
    gather x6 -> x0, local copies, waits for them, and re-layouts: 52.1 us -> none  [the longest x4 34.5 us: local(): chosen = jnp.take(aux_green, sources, axis=0)]
    unnamed x11 -> x0, local copies, waits for them, and re-layouts: 39.6 us -> none
    unnamed x2 -> x0, other arithmetic: 39 us -> none
    convert_element_type x6 -> x0, local copies, waits for them, and re-layouts: 21.6 us -> none  [the longest x2 8.57 us: local(): screen_time[None].astype(jnp.float32)]
  transfers between devices with their start and end apart: 2 -> 0, of which waited for: 2 -> 0; matrix products, arithmetic and copies ran while one was open for 4% -> 0% of each run, Pallas kernels for 0% -> 0%
where the time goes in v2:
time: 126 us
  Pallas kernels  125 us (99%)
  other arithmetic  1.36 us (1%)
    pallas_call x1, Pallas kernels, step(): pl.pallas_call(step_kernel, in_specs=[smem, smem, hbm, hbm, vmem, vmem, v...  120 us
    pallas_call x1, Pallas kernels, sigma(): pl.pallas_call(sigma_kernel, grid_spec=pltpu.PrefetchScalarGridSpec(num_s...  4.37 us

profile of v2, /device:TPU:1, one launch (start us, length us, event | category | flops | bytes accessed | tf_op | source)
XLA Modules:
  0.0 126.2 jit_solution(5110750621914164286)
XLA Ops:
  0.0 1.4 %select_reduce_fusion.source_ref = s32[8,8]{1,0:T(8,128)} fusion(s32[8,8]{1,0:T(8,128)} %kplus_ref.1), kind=kLoop, calls=%fused_computation | loop fusion | flops 1472 | bytes 512 | tf_op jit(solution)/shard_map/reduce_sum | solution.py:331
  1.4 120.5 %step.1 = bf16[3,8,128,256]{3,2,1,0:T(8,128)(2,1)} custom-call(s32[8,8]{1,0:T(8,128)} %kplus_ref.1, s32[8,8]{1,0:T(8,128)} %select_reduce_fusion.source_ref, bf16[8,8,256,256]{3,2,1,0:T(8,128)(2,1)} %green_ref.1, bf16[8,384,256]{2,1,0:T(8,128)(2,1)} %colloc_ref.3, bf16[128,128]{1,0:T(8,128)(2,1)} %freq_ref.1, bf16[128,128]{1,0:T(8,128)(2,1)} %time_ref.1, ...), custom_call_target="tpu_custom_call" | custom-call | tf_op jit(solution)/shard_map/step/pallas_call | solution.py:274
  121.9 4.4 %sigma.1 = f32[1,8,256,256]{3,2,1,0:T(8,128)} custom-call(s32[1]{0:T(128)} %bitcast.place_ref, bf16[3,8,2,64,256]{4,3,2,1,0:T(8,128)(2,1)} %bitcast.2, bf16[8,384,256]{2,1,0:T(8,128)(2,1)} %colloc_ref.3), custom_call_target="tpu_custom_call" | custom-call | tf_op jit(solution)/shard_map/sigma/pallas_call | solution.py:313

commit v3 on v2

--- a/solution.py
+++ b/solution.py
@@ -37,9 +37,9 @@
 
 
 def step_kernel(
-    kplus_ref, source_ref, green_ref, colloc_ref, freq_ref, time_ref, coul_ref, out_ref,
+    kplus_ref, green_ref, colloc_ref, freq_ref, time_ref, coul_ref, out_ref,
     green_s, colloc_s, left_s, right_s, aux_s, mirror_s, polar, times, freqs, whole, chain, back, stamps, screen, wide,
-    sum_s, half_s, load_sem, send_sem, recv_sem, own_sem, last_send, last_recv, last_own,
+    late_wide, sum_s, half_s, source_ref, load_sem, send_sem, recv_sem, own_sem, last_send, last_recv, last_own,
 ):
     pb, ta = lax.axis_index("pb"), lax.axis_index("ta")
     z_hi, z_lo, y, core = pb // 4, ta // 8, lax.rem(ta // 2, 4), lax.rem(ta, 2)
@@ -143,7 +143,7 @@
                 mirror_s[g, k] = mirror[128 * g : 128 * g + 128]
             return carry
 
-        lax.fori_loop(0, NK, widen, 0)
+        lax.fori_loop(0, NK, widen, 0, unroll=True)
         for g in range(GROUPS):
             n = 3 * ch + g
 
@@ -162,13 +162,24 @@
 
             lax.fori_loop(0, 4, polarize, 0)
             send(0, n)
-
-    spread(freq_ref[...], wide)
+        if ch == 0:
+            spread(freq_ref[...], wide)
+
+    def find(i, carry):
+        q, c = i // NK, lax.rem(i, NK)
+        found = jnp.int32(0)
+        for k in range(NK):
+            found = jnp.where(kplus_ref[q, k] == c, k, found)
+        source_ref[q, c] = found
+        return carry
+
     for n in range(PARTS):
         receive(0, n)
         transform(wide, times, freqs, n)
         send(1, n)
-    spread(time_ref[...], wide)
+        if n == PARTS // 2:
+            spread(time_ref[...], late_wide)
+            lax.fori_loop(0, NK * NK, find, 0)
     for n in range(PARTS):
         receive(1, n)
 
@@ -186,10 +197,9 @@
                 axis=1,
             )
             low = full.astype(BF16)
-            first = dot(low, coul).astype(BF16)
-            series = (full + dot(first, low)).astype(BF16)
-            left = dot(coul, series).astype(BF16)
-            screened.append(dot(left, coul))
+            left = dot(coul, low).astype(BF16)
+            bare = dot(left, coul)
+            screened.append(bare + dot(left, bare.astype(BF16)))
         for ch in range(GROUPS):
             for g in range(GROUPS):
                 both = [
@@ -199,46 +209,35 @@
         return carry
 
     order = [3 * ch + g for g in range(GROUPS) for ch in range(GROUPS)]
-    ahead = 3
-    lax.fori_loop(0, 2, pair, 0)
-    for n in order[:ahead]:
-        send(2, n, 0, 32)
-    lax.fori_loop(2, 4, pair, 0)
-    for at, n in enumerate(order):
-        send(2, n, 32, 32)
-        if at + ahead < PARTS:
-            send(2, order[at + ahead], 0, 32)
+    for wp in range(NT // 2):
+        pair(wp, 0)
+    for n in order:
+        send(2, n)
 
     last = []
-    for at, n in enumerate(order):
-        receive(2, n)
-        transform(wide, back, stamps, n)
-        send(3, n)
-    for g in range(GROUPS):
-        for ch in range(GROUPS):
-            n = 3 * ch + g
-            receive(3, n)
-
-            def weigh(i, carry):
-                rows = pl.ds(pl.multiple_of(32 * i, 32), 32)
-                here = pl.ds(pl.multiple_of(32 * lax.rem(i, 2), 32), 32)
-                screens = [screen[n, 2 * q + i // 2, here, :].astype(F32) for q in range(NK)]
-                for c in range(NK):
-                    total = None
-                    for q in range(NK):
-                        term = aux_s[n, source_ref[q, c], rows, :] * screens[q]
-                        total = term if total is None else total + term
-                    sum_s[c, rows, LANES * ch : LANES * ch + LANES] = total.astype(BF16)
-                return carry
-
-            lax.fori_loop(0, 4, weigh, 0)
-
-        def halve(s, carry):
+    def weigh_part(n):
+        ch = n // GROUPS
+
+        def weigh(i, carry):
+            rows = pl.ds(pl.multiple_of(32 * i, 32), 32)
+            here = pl.ds(pl.multiple_of(32 * lax.rem(i, 2), 32), 32)
+            screens = [screen[n, 2 * q + i // 2, here, :].astype(F32) for q in range(NK)]
+            for c in range(NK):
+                total = None
+                for q in range(NK):
+                    term = aux_s[n, source_ref[q, c], rows, :] * screens[q]
+                    total = term if total is None else total + term
+                sum_s[c, rows, LANES * ch : LANES * ch + LANES] = total.astype(BF16)
+            return carry
+
+        lax.fori_loop(0, 4, weigh, 0)
+
+    def halve(g):
+        for s in range(NK):
             c = lax.bitwise_xor(pb, s)
-            half_s[g, c] = dot(sum_s[c], colloc_s[c]).astype(BF16)
-
-            @pl.when(s > 0)
-            def _():
+            product = dot(sum_s[c], colloc_s[c]).reshape(2, NT, 8, 256)
+            half_s[g, c] = jnp.stack([product[0], product[1]], axis=1).reshape(128, 256).astype(BF16)
+            if s:
                 pltpu.make_async_remote_copy(
                     src_ref=half_s.at[g, c],
                     dst_ref=out_ref.at[g, pb],
@@ -247,13 +246,21 @@
                     device_id=(c, ta),
                     device_id_type=MESH,
                 ).start()
-
-            return carry
-
-        lax.fori_loop(0, NK, halve, 0)
         own = pltpu.make_async_copy(half_s.at[g, pb], out_ref.at[g, pb], last_own.at[g])
         own.start()
         last.append(own)
+
+    behind = 6
+    for at in range(PARTS + behind):
+        if at < PARTS:
+            receive(2, order[at])
+            transform(late_wide, back, stamps, order[at])
+            send(3, order[at])
+        if at >= behind:
+            receive(3, order[at - behind])
+            weigh_part(order[at - behind])
+            if (at - behind) % GROUPS == GROUPS - 1:
+                halve((at - behind) // GROUPS)
     for g in range(GROUPS):
         last[g].wait()
         part = out_ref.at[g, pl.ds(0, NK - 1)]
@@ -265,7 +272,7 @@
             sent(stage, n)
 
 
-def step(kplus, sources, green, colloc, to_freq, to_time, coulomb):
+def step(kplus, green, colloc, to_freq, to_time, coulomb):
     block = (PARTS, 16, 64, LANES)
     vmem = pl.BlockSpec(memory_space=pltpu.VMEM)
     smem = pl.BlockSpec(memory_space=pltpu.SMEM)
@@ -273,7 +280,7 @@
     dma = pltpu.SemaphoreType.DMA
     return pl.pallas_call(
         step_kernel,
-        in_specs=[smem, smem, hbm, hbm, vmem, vmem, vmem],
+        in_specs=[smem, hbm, hbm, vmem, vmem, vmem],
         out_specs=hbm,
         out_shape=jax.ShapeDtypeStruct((GROUPS, NK, 128, 256), BF16),
         scratch_shapes=[
@@ -287,8 +294,10 @@
         + [pltpu.VMEM(block, BF16)] * 8
         + [
             pltpu.VMEM((1024, 1024), BF16),
+            pltpu.VMEM((1024, 1024), BF16),
             pltpu.VMEM((NK, 128, 384), BF16),
             pltpu.VMEM((GROUPS, NK, 128, 256), BF16),
+            pltpu.SMEM((NK, NK), jnp.int32),
             dma((NK + 1,)),
             dma((4, PARTS)),
             dma((4, PARTS)),
@@ -299,37 +308,35 @@
         ],
         compiler_params=pltpu.CompilerParams(collective_id=0, has_side_effects=True, vmem_limit_bytes=56 * MIB),
         name="step",
-    )(kplus, sources, green, colloc, to_freq, to_time, coulomb)
+    )(kplus, green, colloc, to_freq, to_time, coulomb)
 
 
 def sigma_kernel(place_ref, half_ref, colloc_ref, out_ref):
-    half = half_ref[...].astype(F32).reshape(GROUPS, NK, 2, 2, 8, 256)
-    for j in range(2):
-        whole = half[:, :, :, j].reshape(384, 256).astype(BF16)
-        out_ref[0, j] = dot(colloc_ref[0], whole, ((0,), (0,))) * (-1.0 / NK)
+    for t in range(out_ref.shape[1]):
+        out_ref[0, t] = dot(colloc_ref[0], half_ref[:, :, t].reshape(384, 256), ((0,), (0,))) * (-1.0 / NK)
 
 
 def sigma(half, colloc, place):
+    size = 4
     return pl.pallas_call(
         sigma_kernel,
         grid_spec=pltpu.PrefetchScalarGridSpec(
             num_scalar_prefetch=1,
-            grid=(NT // 2,),
+            grid=(NT // size,),
             in_specs=[
-                pl.BlockSpec((GROUPS, NK, 2, 16, 256), lambda tp, place: (0, 0, 0, tp, 0)),
-                pl.BlockSpec((1, 384, 256), lambda tp, place: (place[0], 0, 0)),
+                pl.BlockSpec((GROUPS, NK, size, 16, 256), lambda i, place: (0, 0, i, 0, 0)),
+                pl.BlockSpec((1, 384, 256), lambda i, place: (place[0], 0, 0)),
             ],
-            out_specs=pl.BlockSpec((1, 2, 256, 256), lambda tp, place: (0, tp, 0, 0)),
+            out_specs=pl.BlockSpec((1, size, 256, 256), lambda i, place: (0, i, 0, 0)),
         ),
         out_shape=jax.ShapeDtypeStruct((1, NT, 256, 256), F32),
+        compiler_params=pltpu.CompilerParams(vmem_limit_bytes=56 * MIB),
         name="sigma",
-    )(place, half.reshape(GROUPS, NK, 2, 64, 256), colloc)
+    )(place, half.reshape(GROUPS, NK, NT, 16, 256), colloc)
 
 
 def local(green, colloc, kplus, to_freq, to_time, coulomb):
-    points = jnp.arange(NK, dtype=jnp.int32)
-    sources = jnp.sum(jnp.where(kplus[:, :, None] == points[None, None, :], points[None, :, None], 0), axis=1)
-    half = step(kplus, sources, green, colloc, to_freq, to_time, coulomb)
+    half = step(kplus, green, colloc, to_freq, to_time, coulomb)
     return sigma(half, colloc, lax.axis_index("pb").astype(jnp.int32).reshape(1))
 
 

time: 126 us -> 114 us (0.905)
  Pallas kernels: 125 us -> 114 us
  other arithmetic: 1.36 us -> 0 us
    pallas_call x1, Pallas kernels: 120 us -> 111 us  [step(): pl.pallas_call(step_kernel, in_specs=[smem, hbm, hbm, vmem, vmem, vmem],...]
    reduce_sum x1 -> x0, other arithmetic: 1.36 us -> none  [local(): jnp.sum(jnp.where(kplus[:, :, None] == points[None, None, :], points[None...]
where the time goes in v3:
time: 114 us
  Pallas kernels  114 us (100%)
    pallas_call x1, Pallas kernels, step(): pl.pallas_call(step_kernel, in_specs=[smem, hbm, hbm, vmem, vmem, vmem],...  111 us
    pallas_call x1, Pallas kernels, sigma(): pl.pallas_call(sigma_kernel, grid_spec=pltpu.PrefetchScalarGridSpec(num_s...  3.14 us

profile of v3, /device:TPU:1, one launch (start us, length us, event | category | flops | bytes accessed | tf_op | source)
XLA Modules:
  0.0 113.8 jit_solution(13086632165414536787)
XLA Ops:
  0.0 110.7 %step.1 = bf16[3,8,128,256]{3,2,1,0:T(8,128)(2,1)} custom-call(s32[8,8]{1,0:T(8,128)} %kplus_ref.1, bf16[8,8,256,256]{3,2,1,0:T(8,128)(2,1)} %green_ref.1, bf16[8,384,256]{2,1,0:T(8,128)(2,1)} %colloc_ref.3, bf16[128,128]{1,0:T(8,128)(2,1)} %freq_ref.1, bf16[128,128]{1,0:T(8,128)(2,1)} %time_ref.1, bf16[384,384]{1,0:T(8,128)(2,1)} %coul_ref.1), custom_call_target="tpu_custom_call" | custom-call | tf_op jit(solution)/shard_map/step/pallas_call | solution.py:281
  110.7 3.1 %sigma.1 = f32[1,8,256,256]{3,2,1,0:T(8,128)} custom-call(s32[1]{0:T(128)} %bitcast.place_ref, bf16[3,8,8,16,256]{4,3,2,1,0:T(8,128)(2,1)} %bitcast.2, bf16[8,384,256]{2,1,0:T(8,128)(2,1)} %colloc_ref.3), custom_call_target="tpu_custom_call" | custom-call | tf_op jit(solution)/shard_map/sigma/pallas_call | solution.py:321

commit v4 on v3

--- a/solution.py
+++ b/solution.py
@@ -38,65 +38,81 @@
 
 def step_kernel(
     kplus_ref, green_ref, colloc_ref, freq_ref, time_ref, coul_ref, out_ref,
-    green_s, colloc_s, left_s, right_s, aux_s, mirror_s, polar, times, freqs, whole, chain, back, stamps, screen, wide,
+    green_s, colloc_s, rows_s, left_s, right_s, aux_s, mirror_s, polar, times, freqs, whole, chain, back, stamps, screen, wide,
     late_wide, sum_s, half_s, source_ref, load_sem, send_sem, recv_sem, own_sem, last_send, last_recv, last_own,
 ):
     pb, ta = lax.axis_index("pb"), lax.axis_index("ta")
-    z_hi, z_lo, y, core = pb // 4, ta // 8, lax.rem(ta // 2, 4), lax.rem(ta, 2)
-    own_q = y + 4 * lax.bitwise_xor(z_lo, z_hi)
+    z_hi, x = pb >> 2, pb & 3
+    z_lo, y, core = ta >> 3, (ta >> 1) & 3, ta & 1
+    own_q = y + 4 * (z_lo ^ z_hi)
     own_block = 2 * pb + core
 
     def load(k):
         return pltpu.make_async_copy(green_ref.at[k], green_s.at[k], load_sem.at[k])
 
+    def load_rows(g):
+        rows = pl.ds(pl.multiple_of(128 * g + 16 * pb, 16), 16)
+        return pltpu.make_async_copy(colloc_ref.at[:, rows, :], rows_s.at[:, g], load_sem.at[NK + 1 + g])
+
     load_colloc = pltpu.make_async_copy(colloc_ref, colloc_s, load_sem.at[NK])
-    load_colloc.start()
+    for g in range(GROUPS):
+        load_rows(g).start()
     for k in range(NK):
         load(k).start()
-
-    def line(j):
-        return (pb, j)
-
-    def plane(j):
-        other = j // 2
-        other_lo = lax.bitwise_xor(lax.bitwise_xor(z_lo, z_hi), other // 4)
-        return (other, 8 * other_lo + 2 * y + lax.rem(j, 2))
-
-    def transfer_slot(j):
-        return 2 * (lax.rem(j // 2, 4) + 4 * lax.bitwise_xor(j // 8, z_hi)) + lax.rem(j, 2)
-
-    same = lambda j: j
+    load_colloc.start()
+
+    way = 1 - 2 * core
+
+    def split(s, at, z):
+        ring = ((s >> 1) & 1) | ((s >> 3) << 1)
+        return (at + way * ring) & 3, z ^ (s & 1), core ^ ((s >> 2) & 1)
+
+    def line(s):
+        other_y, other_z, other_core = split(s, y, z_lo)
+        return ((other_z << 3) | (other_y << 1) | other_core), (pb, (other_z << 3) | (other_y << 1) | other_core)
+
+    def line_transfer(s):
+        other, device = line(s)
+        return other ^ (z_hi << 3), device
+
+    def plane(s):
+        other_x, other_z, other_core = split(s, x, z_hi)
+        other = (other_z << 2) | other_x
+        return (other << 1) | other_core, (other, ((z_lo ^ z_hi ^ other_z) << 3) | (y << 1) | other_core)
+
+    def last_partner(s):
+        return ((z_hi ^ (s & 1)) << 2) | ((x + way * (s >> 1)) & 3)
+
     stages = (
-        (polar, transfer_slot, times, ta, line, ta),
-        (freqs, same, whole, own_block, plane, own_block),
-        (chain, same, back, own_block, plane, own_block),
-        (stamps, same, screen, 2 * own_q + core, line, ta),
+        (polar, times, ta, line_transfer),
+        (freqs, whole, own_block, plane),
+        (chain, back, own_block, plane),
+        (stamps, screen, 2 * own_q + core, line),
     )
 
-    def send(stage, n, first=0, size=64):
-        src, slot, dst, there, device, me = stages[stage]
-        rows = pl.ds(first, size)
+    def send(stage, n):
+        src, dst, there, partner = stages[stage]
 
         def go(s, carry):
-            j = lax.bitwise_xor(me, s)
+            slot, device = partner(s)
             pltpu.make_async_remote_copy(
-                src_ref=src.at[n, slot(j), rows],
-                dst_ref=dst.at[n, there, rows],
+                src_ref=src.at[n, slot],
+                dst_ref=dst.at[n, there],
                 send_sem=send_sem.at[stage, n],
                 recv_sem=recv_sem.at[stage, n],
-                device_id=device(j),
+                device_id=device,
                 device_id_type=MESH,
             ).start()
             return carry
 
-        lax.fori_loop(1, 16, go, 0)
-        pltpu.make_async_copy(src.at[n, slot(me), rows], dst.at[n, there, rows], own_sem.at[stage, n]).start()
+        lax.fori_loop(1, 16, go, 0, unroll=True)
+        pltpu.make_async_copy(src.at[n, partner(0)[0]], dst.at[n, there], own_sem.at[stage, n]).start()
 
     def receive(stage, n):
-        src, slot, dst, there, device, me = stages[stage]
+        src, dst, there, partner = stages[stage]
         part = dst.at[n, pl.ds(0, 15)]
         pltpu.make_async_copy(part, part, recv_sem.at[stage, n]).wait()
-        pltpu.make_async_copy(src.at[n, slot(me)], dst.at[n, there], own_sem.at[stage, n]).wait()
+        pltpu.make_async_copy(src.at[n, partner(0)[0]], dst.at[n, there], own_sem.at[stage, n]).wait()
 
     def sent(stage, n):
         part = stages[stage][0].at[n, pl.ds(0, 15)]
@@ -105,24 +121,23 @@
     barrier = pltpu.get_barrier_semaphore()
 
     def greet(s, carry):
-        pl.semaphore_signal(barrier, inc=1, device_id=line(lax.bitwise_xor(ta, s)), device_id_type=MESH)
-        pl.semaphore_signal(barrier, inc=1, device_id=plane(lax.bitwise_xor(own_block, s)), device_id_type=MESH)
+        pl.semaphore_signal(barrier, inc=1, device_id=line(s)[1], device_id_type=MESH)
+        pl.semaphore_signal(barrier, inc=1, device_id=plane(s)[1], device_id_type=MESH)
         return carry
 
     def greet_last(s, carry):
-        pl.semaphore_signal(barrier, inc=1, device_id=(lax.bitwise_xor(pb, s), ta), device_id_type=MESH)
+        pl.semaphore_signal(barrier, inc=1, device_id=(pb ^ s, ta), device_id_type=MESH)
         return carry
 
     lax.fori_loop(1, 16, greet, 0)
     lax.fori_loop(1, NK, greet_last, 0)
 
-    load_colloc.wait()
+    for g in range(GROUPS):
+        load_rows(g).wait()
 
     def project(k, carry):
         load(k).wait()
-        rows = jnp.concatenate(
-            [colloc_s[k, pl.ds(pl.multiple_of(128 * g + 16 * pb, 16), 16), :] for g in range(GROUPS)], axis=0
-        )
+        rows = rows_s[k].reshape(48, 256)
         left = [dot(rows, green_s[k, t]).reshape(6, 1, 8, 256) for t in range(NT)]
         right = [dot(rows, green_s[k, t ^ 1], ((1,), (1,))).reshape(6, 1, 8, 256) for t in range(NT)]
         left_s[k] = jnp.concatenate(left, axis=1).reshape(384, 256).astype(BF16)
@@ -130,6 +145,7 @@
         return carry
 
     lax.fori_loop(0, NK, project, 0)
+    load_colloc.wait()
     pl.semaphore_wait(barrier, 30 + NK - 1)
 
     for ch in range(GROUPS):
@@ -187,17 +203,20 @@
         coul = coul_ref[...]
         rows = pl.ds(pl.multiple_of(16 * wp, 16), 16)
         lines = [whole[n, :, rows, :].astype(F32).reshape(16, 2, 8, LANES) for n in range(PARTS)]
-        screened = []
+        full = []
         for j in range(2):
-            full = jnp.concatenate(
+            matrix = jnp.concatenate(
                 [
                     jnp.concatenate([lines[3 * ch + g][:, j].reshape(128, LANES) for g in range(GROUPS)], axis=0)
                     for ch in range(GROUPS)
                 ],
                 axis=1,
             )
-            low = full.astype(BF16)
-            left = dot(coul, low).astype(BF16)
+            full.append(matrix.astype(BF16))
+        lefts = dot(coul, jnp.concatenate(full, axis=1)).astype(BF16)
+        screened = []
+        for j in range(2):
+            left = lefts[:, 384 * j : 384 * j + 384]
             bare = dot(left, coul)
             screened.append(bare + dot(left, bare.astype(BF16)))
         for ch in range(GROUPS):
@@ -234,7 +253,7 @@
 
     def halve(g):
         for s in range(NK):
-            c = lax.bitwise_xor(pb, s)
+            c = last_partner(s)
             product = dot(sum_s[c], colloc_s[c]).reshape(2, NT, 8, 256)
             half_s[g, c] = jnp.stack([product[0], product[1]], axis=1).reshape(128, 256).astype(BF16)
             if s:
@@ -286,6 +305,7 @@
         scratch_shapes=[
             pltpu.VMEM((NK, NT, 256, 256), BF16),
             pltpu.VMEM((NK, 384, 256), BF16),
+            pltpu.VMEM((NK, GROUPS, 16, 256), BF16),
             pltpu.VMEM((NK, 384, 256), BF16),
             pltpu.VMEM((NK, 384, 256), BF16),
             pltpu.VMEM((PARTS, NK, 128, LANES), F32),
@@ -298,7 +318,7 @@
             pltpu.VMEM((NK, 128, 384), BF16),
             pltpu.VMEM((GROUPS, NK, 128, 256), BF16),
             pltpu.SMEM((NK, NK), jnp.int32),
-            dma((NK + 1,)),
+            dma((NK + 1 + GROUPS,)),
             dma((4, PARTS)),
             dma((4, PARTS)),
             dma((4, PARTS)),

time: 114 us -> 112 us (0.982); the launches traced: 114 us -> 111 us
  Pallas kernels: 114 us -> 111 us
    pallas_call x1, Pallas kernels: 111 us -> 107 us  [step(): pl.pallas_call(step_kernel, in_specs=[smem, hbm, hbm, vmem, vmem, vmem],...]
where the time goes in v4:
time: 112 us; the launch traced here: 111 us
  Pallas kernels  111 us (99%)
    pallas_call x1, Pallas kernels, step(): pl.pallas_call(step_kernel, in_specs=[smem, hbm, hbm, vmem, vmem, vmem],...  107 us
    pallas_call x1, Pallas kernels, sigma(): pl.pallas_call(sigma_kernel, grid_spec=pltpu.PrefetchScalarGridSpec(num_s...  3.14 us

profile of v4, /device:TPU:1, one launch (start us, length us, event | category | flops | bytes accessed | tf_op | source)
XLA Modules:
  0.0 110.6 jit_solution(732952810941548353)
XLA Ops:
  0.0 107.4 %step.1 = bf16[3,8,128,256]{3,2,1,0:T(8,128)(2,1)} custom-call(s32[8,8]{1,0:T(8,128)} %kplus_ref.1, bf16[8,8,256,256]{3,2,1,0:T(8,128)(2,1)} %green_ref.1, bf16[8,384,256]{2,1,0:T(8,128)(2,1)} %colloc_ref.3, bf16[128,128]{1,0:T(8,128)(2,1)} %freq_ref.1, bf16[128,128]{1,0:T(8,128)(2,1)} %time_ref.1, bf16[384,384]{1,0:T(8,128)(2,1)} %coul_ref.1), custom_call_target="tpu_custom_call" | custom-call | tf_op jit(solution)/shard_map/step/pallas_call | solution.py:300
  107.4 3.1 %sigma.1 = f32[1,8,256,256]{3,2,1,0:T(8,128)} custom-call(s32[1]{0:T(128)} %bitcast.place_ref, bf16[3,8,8,16,256]{4,3,2,1,0:T(8,128)(2,1)} %bitcast.2, bf16[8,384,256]{2,1,0:T(8,128)(2,1)} %colloc_ref.3), custom_call_target="tpu_custom_call" | custom-call | tf_op jit(solution)/shard_map/sigma/pallas_call | solution.py:341

commit v5 on v4

--- a/solution.py
+++ b/solution.py
@@ -269,7 +269,7 @@
         own.start()
         last.append(own)
 
-    behind = 6
+    behind = 7
     for at in range(PARTS + behind):
         if at < PARTS:
             receive(2, order[at])

time: 112 us -> 112 us (level); the launches traced: 111 us -> 112 us
    pallas_call x1, Pallas kernels: 107 us -> 109 us  [step(): pl.pallas_call(step_kernel, in_specs=[smem, hbm, hbm, vmem, vmem, vmem],...]
where the time goes in v5:
time: 112 us
  Pallas kernels  112 us (100%)
    pallas_call x1, Pallas kernels, step(): pl.pallas_call(step_kernel, in_specs=[smem, hbm, hbm, vmem, vmem, vmem],...  109 us
    pallas_call x1, Pallas kernels, sigma(): pl.pallas_call(sigma_kernel, grid_spec=pltpu.PrefetchScalarGridSpec(num_s...  3.14 us

profile of v5, /device:TPU:1, one launch (start us, length us, event | category | flops | bytes accessed | tf_op | source)
XLA Modules:
  0.0 111.7 jit_solution(3689614171691584950)
XLA Ops:
  0.0 108.6 %step.1 = bf16[3,8,128,256]{3,2,1,0:T(8,128)(2,1)} custom-call(s32[8,8]{1,0:T(8,128)} %kplus_ref.1, bf16[8,8,256,256]{3,2,1,0:T(8,128)(2,1)} %green_ref.1, bf16[8,384,256]{2,1,0:T(8,128)(2,1)} %colloc_ref.3, bf16[128,128]{1,0:T(8,128)(2,1)} %freq_ref.1, bf16[128,128]{1,0:T(8,128)(2,1)} %time_ref.1, bf16[384,384]{1,0:T(8,128)(2,1)} %coul_ref.1), custom_call_target="tpu_custom_call" | custom-call | tf_op jit(solution)/shard_map/step/pallas_call | solution.py:300
  108.6 3.1 %sigma.1 = f32[1,8,256,256]{3,2,1,0:T(8,128)} custom-call(s32[1]{0:T(128)} %bitcast.place_ref, bf16[3,8,8,16,256]{4,3,2,1,0:T(8,128)(2,1)} %bitcast.2, bf16[8,384,256]{2,1,0:T(8,128)(2,1)} %colloc_ref.3), custom_call_target="tpu_custom_call" | custom-call | tf_op jit(solution)/shard_map/sigma/pallas_call | solution.py:341

commit v6 on v5

--- a/solution.py
+++ b/solution.py
@@ -39,7 +39,7 @@
 def step_kernel(
     kplus_ref, green_ref, colloc_ref, freq_ref, time_ref, coul_ref, out_ref,
     green_s, colloc_s, rows_s, left_s, right_s, aux_s, mirror_s, polar, times, freqs, whole, chain, back, stamps, screen, wide,
-    late_wide, sum_s, half_s, source_ref, load_sem, send_sem, recv_sem, own_sem, last_send, last_recv, last_own,
+    late_wide, sum_s, early_s, half_s, source_ref, load_sem, send_sem, recv_sem, own_sem, last_send, last_recv, last_own,
 ):
     pb, ta = lax.axis_index("pb"), lax.axis_index("ta")
     z_hi, x = pb >> 2, pb & 3
@@ -254,7 +254,8 @@
     def halve(g):
         for s in range(NK):
             c = last_partner(s)
-            product = dot(sum_s[c], colloc_s[c]).reshape(2, NT, 8, 256)
+            product = early_s[c] + dot(sum_s[c, :, 256:384], colloc_s[c, 256:384, :])
+            product = product.reshape(2, NT, 8, 256)
             half_s[g, c] = jnp.stack([product[0], product[1]], axis=1).reshape(128, 256).astype(BF16)
             if s:
                 pltpu.make_async_remote_copy(
@@ -278,6 +279,9 @@
         if at >= behind:
             receive(3, order[at - behind])
             weigh_part(order[at - behind])
+            if (at - behind) % GROUPS == GROUPS - 2:
+                for c in range(NK):
+                    early_s[c] = dot(sum_s[c, :, :256], colloc_s[c, :256, :])
             if (at - behind) % GROUPS == GROUPS - 1:
                 halve((at - behind) // GROUPS)
     for g in range(GROUPS):
@@ -316,6 +320,7 @@
             pltpu.VMEM((1024, 1024), BF16),
             pltpu.VMEM((1024, 1024), BF16),
             pltpu.VMEM((NK, 128, 384), BF16),
+            pltpu.VMEM((NK, 128, 256), F32),
             pltpu.VMEM((GROUPS, NK, 128, 256), BF16),
             pltpu.SMEM((NK, NK), jnp.int32),
             dma((NK + 1 + GROUPS,)),

time: 112 us -> 112 us (level)
  no operation moved by 1% of the time
where the time goes in v6:
time: 112 us
  Pallas kernels  112 us (100%)
    pallas_call x1, Pallas kernels, step(): pl.pallas_call(step_kernel, in_specs=[smem, hbm, hbm, vmem, vmem, vmem],...  109 us
    pallas_call x1, Pallas kernels, sigma(): pl.pallas_call(sigma_kernel, grid_spec=pltpu.PrefetchScalarGridSpec(num_s...  3.14 us

profile of v6, /device:TPU:1, one launch (start us, length us, event | category | flops | bytes accessed | tf_op | source)
XLA Modules:
  0.0 111.7 jit_solution(6360224485656815550)
XLA Ops:
  0.0 108.5 %step.1 = bf16[3,8,128,256]{3,2,1,0:T(8,128)(2,1)} custom-call(s32[8,8]{1,0:T(8,128)} %kplus_ref.1, bf16[8,8,256,256]{3,2,1,0:T(8,128)(2,1)} %green_ref.1, bf16[8,384,256]{2,1,0:T(8,128)(2,1)} %colloc_ref.3, bf16[128,128]{1,0:T(8,128)(2,1)} %freq_ref.1, bf16[128,128]{1,0:T(8,128)(2,1)} %time_ref.1, bf16[384,384]{1,0:T(8,128)(2,1)} %coul_ref.1), custom_call_target="tpu_custom_call" | custom-call | tf_op jit(solution)/shard_map/step/pallas_call | solution.py:304
  108.5 3.1 %sigma.1 = f32[1,8,256,256]{3,2,1,0:T(8,128)} custom-call(s32[1]{0:T(128)} %bitcast.place_ref, bf16[3,8,8,16,256]{4,3,2,1,0:T(8,128)(2,1)} %bitcast.2, bf16[8,384,256]{2,1,0:T(8,128)(2,1)} %colloc_ref.3), custom_call_target="tpu_custom_call" | custom-call | tf_op jit(solution)/shard_map/sigma/pallas_call | solution.py:346
